TPU v7x, 256 devices: a whole 4x4x8 slice. The times are simulated.
256 devices in a mesh: expert: 32 (over z, y), dp: 8 (over x, core).
Axes of the slice: x: 4, y: 4, z: 8, core: 2. Of those that a mesh axis runs over, the one named last changes fastest.
Arguments:
- tokens: bfloat16 [4096, 7168], P(('expert', 'dp')), may hold values from -6 to 6
- grad_out: bfloat16 [4096, 7168], P(('expert', 'dp')), may hold values from -4 to 4
- routes: int32 [4096, 8], P(('expert', 'dp')), may hold values from 0 to 31, all different within a row; in each aligned block of 16 rows (0 to 15, 16 to 31, ...) at most 5 rows name the same one
- gates: bfloat16 [4096, 8], P(('expert', 'dp')), may hold values from 0.049804688 to 0.5
- w_up: bfloat16 [32, 7168, 1024], P('expert', 'dp'), may hold values from -0.0625 to 0.0625
- w_down: bfloat16 [32, 1024, 7168], P('expert', None, 'dp'), may hold values from -0.1875 to 0.1875
Outputs:
- grad_tokens: bfloat16 [4096, 7168], P(('expert', 'dp'))
- grad_gates: float32 [4096, 8], P(('expert', 'dp'))
- grad_up: bfloat16 [32, 7168, 1024], P('expert', 'dp')
- grad_down: bfloat16 [32, 1024, 7168], P('expert', None, 'dp')
Inputs may be any that keep to these rules, and one draw needn't show every extreme that they name: `routes`: each row names 8 different experts. Within the 16 rows of one device no expert is named by more than 5 rows, and in every draw some expert is named exactly 5 times by the rows of some device.
All inputs are finite; a program needn't handle non-finite values.
Results may differ from a plain program's by a relative error of at most 0.023.
Values may be sent and summed in bfloat16 or wider, within the bound.
A program may use at most 128 MiB of HBM per device.

v0:
```python
import jax
import jax.numpy as jnp
from jax import lax
from jax.sharding import PartitionSpec as P


def silu_slope(values):
    sigma = jax.nn.sigmoid(values)
    return sigma * (1.0 + values * (1.0 - sigma))


def local(tokens, grad_out, routes, gates, w_up, w_down):
    tok_rows, top_count = routes.shape
    model_width = tokens.shape[1]
    n_expert = lax.axis_size("expert")
    n_group = lax.axis_size("dp")
    feat_width = model_width // n_group
    capacity = min(
        tok_rows, max(2, tok_rows * top_count // n_expert + tok_rows * top_count // (4 * n_expert))
    )
    slot_count = n_expert * capacity
    row_count = slot_count * n_group
    contract_rows = (((0,), (0,)), ((), ()))
    contract_cols = (((1,), (1,)), ((), ()))
    highest = lax.Precision.HIGHEST
    flat_routes = routes.reshape(tok_rows * top_count)
    onehot = (flat_routes[:, None] == jnp.arange(n_expert, dtype=jnp.int32)[None, :]).astype(
        jnp.int32
    )
    rank_table = jnp.cumsum(onehot, axis=0) - onehot
    rank_of = jnp.sum(rank_table * onehot, axis=1)
    slot_of = flat_routes * capacity + rank_of
    placed = slot_of[:, None] == jnp.arange(slot_count, dtype=jnp.int32)[None, :]
    placed_f = placed.astype(jnp.float32)
    token_slots = jnp.any(placed.reshape(tok_rows, top_count, slot_count), axis=1)
    token_mat = token_slots.astype(jnp.bfloat16)
    sent_inputs = lax.dot_general(
        token_mat, tokens, contract_rows, preferred_element_type=jnp.float32
    ).astype(jnp.bfloat16)
    sent_grads = lax.dot_general(
        token_mat, grad_out, contract_rows, preferred_element_type=jnp.float32
    ).astype(jnp.bfloat16)
    sent_gates = lax.dot_general(
        placed_f,
        gates.reshape(tok_rows * top_count).astype(jnp.float32),
        contract_rows,
        precision=highest,
    ).astype(jnp.bfloat16)
    gate_block = jnp.broadcast_to(
        sent_gates.reshape(n_expert, capacity, 1), (n_expert, capacity, n_group)
    )
    arrived = (
        lax.all_to_all(
            lax.all_to_all(
                sent_inputs.reshape(n_expert, capacity, n_group, feat_width),
                "expert",
                split_axis=0,
                concat_axis=0,
                tiled=True,
            ),
            "dp",
            split_axis=2,
            concat_axis=2,
            tiled=True,
        ),
        lax.all_to_all(
            lax.all_to_all(
                sent_grads.reshape(n_expert, capacity, n_group, feat_width),
                "expert",
                split_axis=0,
                concat_axis=0,
                tiled=True,
            ),
            "dp",
            split_axis=2,
            concat_axis=2,
            tiled=True,
        ),
        lax.all_to_all(
            lax.all_to_all(gate_block, "expert", split_axis=0, concat_axis=0, tiled=True),
            "dp",
            split_axis=2,
            concat_axis=2,
            tiled=True,
        ),
    )
    in_rows = arrived[0].reshape(row_count, feat_width)
    grad_rows = arrived[1].reshape(row_count, feat_width)
    gate_rows = arrived[2].reshape(row_count)
    scaled = (gate_rows.astype(jnp.float32)[:, None] * grad_rows.astype(jnp.float32)).astype(
        jnp.bfloat16
    )
    up_weight = w_up[0]
    down_weight = w_down[0]
    pre_share = lax.psum_scatter(
        jnp.dot(in_rows, up_weight, preferred_element_type=jnp.float32).astype(jnp.bfloat16),
        "dp",
        scatter_dimension=0,
        tiled=True,
    ).astype(jnp.float32)
    hidden_share = jax.nn.silu(pre_share).astype(jnp.bfloat16)
    shard_rows = lax.all_gather(hidden_share, "dp", axis=0, tiled=True)
    expert_out = jnp.dot(shard_rows, down_weight, preferred_element_type=jnp.float32)
    gate_dots = jnp.sum(expert_out * grad_rows.astype(jnp.float32), axis=1)
    down_acc = lax.dot_general(
        shard_rows, scaled, contract_rows, preferred_element_type=jnp.float32
    )
    down_acc, gate_dots = (down_acc, gate_dots)
    back_share = lax.psum_scatter(
        lax.dot_general(
            scaled, down_weight, contract_cols, preferred_element_type=jnp.float32
        ).astype(jnp.bfloat16),
        "dp",
        scatter_dimension=0,
        tiled=True,
    ).astype(jnp.float32)
    slope_share = (back_share * silu_slope(pre_share)).astype(jnp.bfloat16)
    shard_rows = lax.all_gather(slope_share, "dp", axis=0, tiled=True)
    up_acc = lax.dot_general(in_rows, shard_rows, contract_rows, preferred_element_type=jnp.float32)
    input_grads = lax.dot_general(
        shard_rows, up_weight, contract_cols, preferred_element_type=jnp.float32
    )
    up_acc, input_grads = (up_acc, input_grads)
    returned = (
        lax.all_to_all(
            lax.all_to_all(
                input_grads.reshape(n_expert, capacity, n_group, feat_width).astype(jnp.bfloat16),
                "expert",
                split_axis=0,
                concat_axis=0,
                tiled=True,
            ),
            "dp",
            split_axis=2,
            concat_axis=2,
            tiled=True,
        ).astype(jnp.float32),
        lax.all_to_all(
            lax.all_to_all(
                gate_dots.reshape(n_expert, capacity, n_group).astype(jnp.bfloat16),
                "expert",
                split_axis=0,
                concat_axis=0,
                tiled=True,
            ),
            "dp",
            split_axis=2,
            concat_axis=2,
            tiled=True,
        ).astype(jnp.float32),
    )
    slot_grads = returned[0].reshape(slot_count, model_width)
    slot_dots = jnp.sum(returned[1], axis=2).reshape(slot_count)
    token_grads = jnp.dot(token_slots.astype(jnp.float32), slot_grads, precision=highest)
    gate_grads = jnp.dot(placed_f, slot_dots, precision=highest).reshape(tok_rows, top_count)
    return (
        token_grads.astype(jnp.bfloat16),
        gate_grads,
        up_acc.astype(jnp.bfloat16)[None],
        down_acc.astype(jnp.bfloat16)[None],
    )


def solution(mesh):
    return jax.shard_map(
        local,
        mesh=mesh,
        in_specs=(
            P(("expert", "dp"), None),
            P(("expert", "dp"), None),
            P(("expert", "dp"), None),
            P(("expert", "dp"), None),
            P("expert", "dp", None),
            P("expert", None, "dp"),
        ),
        out_specs=(
            P(("expert", "dp"), None),
            P(("expert", "dp"), None),
            P("expert", "dp", None),
            P("expert", None, "dp"),
        ),
        check_vma=False,
    )
```

profile of v0, /device:TPU:1, one launch (start us, length us, event | category | flops | bytes accessed | tf_op | source)
XLA Modules:
  0.0 452.7 jit_solution(8375176513298098135)
XLA Ops:
  10.5 12.0 %all-to-all-start = ((bf16[32,5,8]{1,2,0:T(8,128)(2,1)}), bf16[32,5,8]{1,2,0:T(8,128)(2,1)S(1)}, u32[]{:S(2)}, u32[]{:S(2)}) async-start(bf16[32,5,8]{1,2,0:T(8,128)(2,1)} %broadcast_in_dim.18), calls=%async_computation | async-start | bytes 131072 | tf_op jit(solution)/shard_map/all_to_all | solution.py:80
  26.3 5.0 %all-to-all-done = bf16[32,5,8]{1,2,0:T(8,128)(2,1)S(1)} async-done(((bf16[32,5,8]{1,2,0:T(8,128)(2,1)}), bf16[32,5,8]{1,2,0:T(8,128)(2,1)S(1)}, u32[]{:S(2)}, u32[]{:S(2)}) %all-to-all-start) | async-done | bytes 2592 | tf_op jit(solution)/shard_map/all_to_all | solution.py:80
  31.3 4.8 %all-to-all-start.2 = ((bf16[32,5,8,896]{3,2,1,0:T(8,128)(2,1)}), bf16[32,5,8,896]{3,2,1,0:T(8,128)(2,1)}, u32[]{:S(2)}, u32[]{:S(2)}) async-start(bf16[32,5,8,896]{3,2,1,0:T(8,128)(2,1)} %bitcast.56), calls=%async_computation.2 | async-start | bytes 4587520 | tf_op jit(solution)/shard_map/all_to_all | solution.py:67
  36.9 50.9 %all-to-all-done.2 = bf16[32,5,8,896]{3,2,1,0:T(8,128)(2,1)} async-done(((bf16[32,5,8,896]{3,2,1,0:T(8,128)(2,1)}), bf16[32,5,8,896]{3,2,1,0:T(8,128)(2,1)}, u32[]{:S(2)}, u32[]{:S(2)}) %all-to-all-start.2) | async-done | bytes 2293792 | tf_op jit(solution)/shard_map/all_to_all | solution.py:67
  87.7 8.7 %all-to-all-start.1 = ((bf16[32,5,8]{0,1,2:T(8,128)(2,1)}), bf16[32,5,8]{0,1,2:T(8,128)(2,1)S(1)}, u32[]{:S(2)}, u32[]{:S(2)}) async-start(bf16[32,5,8]{0,1,2:T(8,128)(2,1)} %copy.77), calls=%async_computation.1 | async-start | bytes 32768 | tf_op jit(solution)/shard_map/all_to_all | solution.py:79
  101.1 5.0 %all-to-all-start.3 = ((bf16[32,5,8,896]{3,0,1,2:T(8,128)(2,1)}), bf16[32,5,8,896]{3,0,1,2:T(8,128)(2,1)}, u32[]{:S(2)}, u32[]{:S(2)}) async-start(bf16[32,5,8,896]{3,0,1,2:T(8,128)(2,1)} %copy.80), calls=%async_computation.3 | async-start | bytes 4587520 | tf_op jit(solution)/shard_map/all_to_all | solution.py:66
  108.7 25.9 %all-to-all-done.3 = bf16[32,5,8,896]{3,0,1,2:T(8,128)(2,1)} async-done(((bf16[32,5,8,896]{3,0,1,2:T(8,128)(2,1)}), bf16[32,5,8,896]{3,0,1,2:T(8,128)(2,1)}, u32[]{:S(2)}, u32[]{:S(2)}) %all-to-all-start.3) | async-done | bytes 2293792 | tf_op jit(solution)/shard_map/all_to_all | solution.py:66
  134.6 5.1 %all-to-all-start.4 = ((bf16[32,5,8,896]{3,2,1,0:T(8,128)(2,1)}), bf16[32,5,8,896]{3,2,1,0:T(8,128)(2,1)}, u32[]{:S(2)}, u32[]{:S(2)}) async-start(bf16[32,5,8,896]{3,2,1,0:T(8,128)(2,1)} %bitcast.55), calls=%async_computation.5 | async-start | bytes 4587520 | tf_op jit(solution)/shard_map/all_to_all | solution.py:54
  146.8 45.4 %all-to-all-done.4 = bf16[32,5,8,896]{3,2,1,0:T(8,128)(2,1)} async-done(((bf16[32,5,8,896]{3,2,1,0:T(8,128)(2,1)}), bf16[32,5,8,896]{3,2,1,0:T(8,128)(2,1)}, u32[]{:S(2)}, u32[]{:S(2)}) %all-to-all-start.4) | async-done | bytes 2293792 | tf_op jit(solution)/shard_map/all_to_all | solution.py:54
  194.1 33.9 %all_to_all.50 = bf16[32,5,8,896]{3,0,1,2:T(8,128)(2,1)S(1)} all-to-all(bf16[32,5,8,896]{3,0,1,2:T(8,128)(2,1)S(1)} %copy.82), channel_id=1, replica_groups=mesh['expert'=32,'dp'=8] {'dp'}, dimensions={2} | all-to-all | bytes 4587520 | tf_op jit(solution)/shard_map/all_to_all | solution.py:53
  234.4 30.5 %reduce-scatter.5.cloned.1.call-done = bf16[160,1024]{1,0:T(8,128)(2,1)} async-done(((bf16[1280,1024]{1,0:T(8,128)(2,1)}), bf16[160,1024]{1,0:T(8,128)(2,1)}) %reduce-scatter.5.cloned.1.call-update) | async-done | bytes 327696 | tf_op jit(solution)/shard_map/reduce_scatter | solution.py:95
  267.7 4.5 copy_convert_fusion
  272.2 5.7 %copy.86 = f32[1280,896]{0,1:T(8,128)} copy(f32[1280,896]{1,0:T(8,128)} %bitcast.51) | data formatting | bytes 9175040 | tf_op jit(solution)/shard_map/convert_element_type | solution.py:90
  277.9 20.0 %all-gather.5.cloned.1.call-done = bf16[1280,1024]{1,0:T(8,128)(2,1)} async-done(((bf16[160,1024]{1,0:T(8,128)(2,1)}), bf16[1280,1024]{1,0:T(8,128)(2,1)}) %all-gather.5.cloned.1.call-update) | async-done | bytes 2621456 | tf_op jit(solution)/shard_map/all_gather | solution.py:102
  297.9 6.3 %multiply_reduce_fusion = bf16[1280]{0:T(1024)(128)(2,1)S(1)} fusion(f32[1280,896]{0,1:T(8,128)} %copy.86, bf16[1280,1024]{1,0:T(8,128)(2,1)} %all-gather.5.cloned.1.call-done, bf16[1,1024,896]{2,1,0:T(8,128)(2,1)} %param.11), kind=kOutput, calls=%fused_computation.4 | convolution fusion | flops 2351102720 | bytes 9046528 | tf_op jit(solution)/shard_map/dot_general | solution.py:103
  304.9 9.6 %all-to-all-start.8 = ((bf16[32,5,8]{2,1,0:T(8,128)(2,1)}), bf16[32,5,8]{2,1,0:T(8,128)(2,1)S(1)}, u32[]{:S(2)}, u32[]{:S(2)}) async-start(bf16[32,5,8]{2,1,0:T(8,128)(2,1)} %convert_element_type.106), calls=%async_computation.10 | async-start | bytes 131072 | tf_op jit(solution)/shard_map/all_to_all | solution.py:139
  314.5 14.9 %all-gather.3.cloned.1.call-done = bf16[1280,1024]{1,0:T(8,128)(2,1)} async-done(((bf16[160,1024]{1,0:T(8,128)(2,1)}), bf16[1280,1024]{1,0:T(8,128)(2,1)}) %all-gather.3.cloned.1.call-update) | async-done | bytes 2621456 | tf_op jit(solution)/shard_map/all_gather | solution.py:118
  329.4 6.1 %convolution_convert_fusion.5 = bf16[32,5,8,896]{3,2,1,0:T(8,128)(2,1)} fusion(bf16[32,5,8,1024]{3,2,1,0:T(8,128)(2,1)} %bitcast.65, bf16[1,896,1024]{2,1,0:T(8,128)(2,1)S(1)} %copy-done), kind=kOutput, calls=%fused_computation.11 | convolution fusion | flops 2349957120 | bytes 6750208 | tf_op jit(solution)/shard_map/dot_general | solution.py:120
  335.5 9.7 %all-to-all-start.6 = ((bf16[32,5,8,896]{3,2,1,0:T(8,128)(2,1)}), bf16[32,5,8,896]{3,2,1,0:T(8,128)(2,1)}, u32[]{:S(2)}, u32[]{:S(2)}) async-start(bf16[32,5,8,896]{3,2,1,0:T(8,128)(2,1)} %convolution_convert_fusion.5), calls=%async_computation.8 | async-start | bytes 4587520 | tf_op jit(solution)/shard_map/all_to_all | solution.py:126
  345.9 51.7 %all-to-all-done.6 = bf16[32,5,8,896]{3,2,1,0:T(8,128)(2,1)} async-done(((bf16[32,5,8,896]{3,2,1,0:T(8,128)(2,1)}), bf16[32,5,8,896]{3,2,1,0:T(8,128)(2,1)}, u32[]{:S(2)}, u32[]{:S(2)}) %all-to-all-start.6) | async-done | bytes 2293792 | tf_op jit(solution)/shard_map/all_to_all | solution.py:126
  397.6 6.3 %all-to-all-start.9 = ((bf16[32,5,8]{0,1,2:T(8,128)(2,1)}), bf16[32,5,8]{0,1,2:T(8,128)(2,1)S(1)}, u32[]{:S(2)}, u32[]{:S(2)}) async-start(bf16[32,5,8]{0,1,2:T(8,128)(2,1)} %copy.87), calls=%async_computation.11 | async-start | bytes 32768 | tf_op jit(solution)/shard_map/all_to_all | solution.py:138
  408.6 5.1 %all-to-all-start.7 = ((bf16[32,5,8,896]{3,0,1,2:T(8,128)(2,1)}), bf16[32,5,8,896]{3,0,1,2:T(8,128)(2,1)}, u32[]{:S(2)}, u32[]{:S(2)}) async-start(bf16[32,5,8,896]{3,0,1,2:T(8,128)(2,1)} %copy.84), calls=%async_computation.9 | async-start | bytes 4587520 | tf_op jit(solution)/shard_map/all_to_all | solution.py:125
  413.9 6.4 %convert_bitcast_fusion.1 = bf16[1,896,1024]{2,1,0:T(8,128)(2,1)} fusion(bf16[1280,896]{1,0:T(8,128)(2,1)} %bitcast.62, bf16[1280,1024]{1,0:T(8,128)(2,1)} %all-gather.3.cloned.1.call-done), kind=kOutput, calls=%fused_computation.17 | convolution fusion | flops 2349727744 | bytes 6750208 | tf_op jit(solution)/shard_map/dot_general | solution.py:119
  426.0 16.3 %all-to-all-done.7 = bf16[32,5,8,896]{3,0,1,2:T(8,128)(2,1)} async-done(((bf16[32,5,8,896]{3,0,1,2:T(8,128)(2,1)}), bf16[32,5,8,896]{3,0,1,2:T(8,128)(2,1)}, u32[]{:S(2)}, u32[]{:S(2)}) %all-to-all-start.7) | async-done | bytes 2293792 | tf_op jit(solution)/shard_map/all_to_all | solution.py:125
  (69 shorter events, 48.9 us)
Async XLA Ops:
  7.2 223.0 %copy-start = (bf16[1,896,1024]{2,1,0:T(8,128)(2,1)S(1)}, bf16[1,896,1024]{2,1,0:T(8,128)(2,1)}, u32[]{:S(2)}) copy-start(bf16[1,896,1024]{2,1,0:T(8,128)(2,1)} %param.10) | copy-start | bytes 5505028
  10.5 20.9 %all-to-all-start = ((bf16[32,5,8]{1,2,0:T(8,128)(2,1)}), bf16[32,5,8]{1,2,0:T(8,128)(2,1)S(1)}, u32[]{:S(2)}, u32[]{:S(2)}) async-start(bf16[32,5,8]{1,2,0:T(8,128)(2,1)} %broadcast_in_dim.18), calls=%async_computation | async-start | bytes 131072 | tf_op jit(solution)/shard_map/all_to_all | solution.py:80
  31.3 56.4 %all-to-all-start.2 = ((bf16[32,5,8,896]{3,2,1,0:T(8,128)(2,1)}), bf16[32,5,8,896]{3,2,1,0:T(8,128)(2,1)}, u32[]{:S(2)}, u32[]{:S(2)}) async-start(bf16[32,5,8,896]{3,2,1,0:T(8,128)(2,1)} %bitcast.56), calls=%async_computation.2 | async-start | bytes 4587520 | tf_op jit(solution)/shard_map/all_to_all | solution.py:67
  87.7 13.3 %all-to-all-start.1 = ((bf16[32,5,8]{0,1,2:T(8,128)(2,1)}), bf16[32,5,8]{0,1,2:T(8,128)(2,1)S(1)}, u32[]{:S(2)}, u32[]{:S(2)}) async-start(bf16[32,5,8]{0,1,2:T(8,128)(2,1)} %copy.77), calls=%async_computation.1 | async-start | bytes 32768 | tf_op jit(solution)/shard_map/all_to_all | solution.py:79
  99.8 6.3 %copy-start.2 = (bf16[16,7168]{1,0:T(8,128)(2,1)S(1)}, bf16[16,7168]{1,0:T(8,128)(2,1)}, u32[]{:S(2)}) copy-start(bf16[16,7168]{1,0:T(8,128)(2,1)} %param.6) | copy-start | bytes 688132
  101.1 33.5 %all-to-all-start.3 = ((bf16[32,5,8,896]{3,0,1,2:T(8,128)(2,1)}), bf16[32,5,8,896]{3,0,1,2:T(8,128)(2,1)}, u32[]{:S(2)}, u32[]{:S(2)}) async-start(bf16[32,5,8,896]{3,0,1,2:T(8,128)(2,1)} %copy.80), calls=%async_computation.3 | async-start | bytes 4587520 | tf_op jit(solution)/shard_map/all_to_all | solution.py:66
  134.6 57.6 %all-to-all-start.4 = ((bf16[32,5,8,896]{3,2,1,0:T(8,128)(2,1)}), bf16[32,5,8,896]{3,2,1,0:T(8,128)(2,1)}, u32[]{:S(2)}, u32[]{:S(2)}) async-start(bf16[32,5,8,896]{3,2,1,0:T(8,128)(2,1)} %bitcast.55), calls=%async_computation.5 | async-start | bytes 4587520 | tf_op jit(solution)/shard_map/all_to_all | solution.py:54
  139.7 94.7 %reduce-scatter.3.cloned.1.call-start = ((), (), s32[]{:S(2)}) async-start(), calls=%async_computation.12 | async-start | bytes 2949120 | tf_op jit(solution)/shard_map/reduce_scatter | solution.py:109
  139.9 2.5 copy-start.4
  146.7 118.2 %reduce-scatter.5.cloned.1.call-start = ((), (), s32[]{:S(2)}) async-start(), calls=%async_computation.13 | async-start | bytes 2949120 | tf_op jit(solution)/shard_map/reduce_scatter | solution.py:95
  228.8 1.4 copy-start.1
  234.3 63.6 %all-gather.5.cloned.1.call-start = ((), (), s32[]{:S(2)}) async-start(), calls=%async_computation.15 | async-start | bytes 2949120 | tf_op jit(solution)/shard_map/all_gather | solution.py:102
  267.1 62.3 %all-gather.3.cloned.1.call-start = ((), (), s32[]{:S(2)}) async-start(), calls=%async_computation.14 | async-start | bytes 2949120 | tf_op jit(solution)/shard_map/all_gather | solution.py:118
  304.9 30.6 %all-to-all-start.8 = ((bf16[32,5,8]{2,1,0:T(8,128)(2,1)}), bf16[32,5,8]{2,1,0:T(8,128)(2,1)S(1)}, u32[]{:S(2)}, u32[]{:S(2)}) async-start(bf16[32,5,8]{2,1,0:T(8,128)(2,1)} %convert_element_type.106), calls=%async_computation.10 | async-start | bytes 131072 | tf_op jit(solution)/shard_map/all_to_all | solution.py:139
  335.5 62.1 %all-to-all-start.6 = ((bf16[32,5,8,896]{3,2,1,0:T(8,128)(2,1)}), bf16[32,5,8,896]{3,2,1,0:T(8,128)(2,1)}, u32[]{:S(2)}, u32[]{:S(2)}) async-start(bf16[32,5,8,896]{3,2,1,0:T(8,128)(2,1)} %convolution_convert_fusion.5), calls=%async_computation.8 | async-start | bytes 4587520 | tf_op jit(solution)/shard_map/all_to_all | solution.py:126
  397.6 11.0 %all-to-all-start.9 = ((bf16[32,5,8]{0,1,2:T(8,128)(2,1)}), bf16[32,5,8]{0,1,2:T(8,128)(2,1)S(1)}, u32[]{:S(2)}, u32[]{:S(2)}) async-start(bf16[32,5,8]{0,1,2:T(8,128)(2,1)} %copy.87), calls=%async_computation.11 | async-start | bytes 32768 | tf_op jit(solution)/shard_map/all_to_all | solution.py:138
  408.6 11.6 %slice-start = ((s8[4587520]{0:T(1024)(128)(4,1)}), s8[393216]{0:T(1024)(128)(4,1)S(1)}, s32[]{:S(2)}) async-start(s8[4587520]{0:T(1024)(128)(4,1)} %bitcast.52), calls=%async_computation.16 | async-start | bytes 786432
  408.6 33.7 %all-to-all-start.7 = ((bf16[32,5,8,896]{3,0,1,2:T(8,128)(2,1)}), bf16[32,5,8,896]{3,0,1,2:T(8,128)(2,1)}, u32[]{:S(2)}, u32[]{:S(2)}) async-start(bf16[32,5,8,896]{3,0,1,2:T(8,128)(2,1)} %copy.84), calls=%async_computation.9 | async-start | bytes 4587520 | tf_op jit(solution)/shard_map/all_to_all | solution.py:125
  413.8 6.4 %slice-start.1 = ((s8[4587520]{0:T(1024)(128)(4,1)}), s8[4194304]{0:T(1024)(128)(4,1)S(1)}, s32[]{:S(2)}) async-start(s8[4587520]{0:T(1024)(128)(4,1)} %bitcast.52), calls=%async_computation.17 | async-start | bytes 8388608
  413.8 6.4 %copy-start.3 = (bf16[1280,1024]{1,0:T(8,128)(2,1)S(1)}, bf16[1280,1024]{1,0:T(8,128)(2,1)}, u32[]{:S(2)}) copy-start(bf16[1280,1024]{1,0:T(8,128)(2,1)} %all-gather.5.cloned.1.call-done) | copy-start | bytes 7864324
Sparse Core Ops, SparseCore 0:
  146.9 35.2 reduce-scatter.2
  234.4 30.4 reduce-scatter.4
  267.3 30.5 all-gather.4
  300.2 29.2 all-gather.2
where the time goes:
time: 454 us; the launch traced here: 453 us
  waiting for transfers between devices  264 us (58%)
  starting transfers between devices  66.6 us (15%)
  matrix products  35.8 us (8%)
  blocking collectives  33.9 us (7%)
  local copies, waits for them, and re-layouts  28.9 us (6%)
  between operations  14 us (3%)
  other arithmetic  9.81 us (2%)
    all_to_all x1, waiting for transfers between devices, local(): lax.all_to_all(input_grads.reshape(n_expert, capacity, n_group, feat_widt...  51.7 us
    all_to_all x1, waiting for transfers between devices, local(): lax.all_to_all(sent_grads.reshape(n_expert, capacity, n_group, feat_width...  50.9 us
    all_to_all x1, waiting for transfers between devices, local(): lax.all_to_all(sent_inputs.reshape(n_expert, capacity, n_group, feat_widt...  45.4 us
    all_to_all x1, blocking collectives, local(): lax.all_to_all(lax.all_to_all(sent_inputs.reshape(n_expert, capacity, n_g...  33.9 us
    reduce_scatter x1, waiting for transfers between devices, local(): lax.psum_scatter(jnp.dot(in_rows, up_weight, preferred_element_type=jnp.f...  30.5 us
    all_to_all x1, waiting for transfers between devices, local(): lax.all_to_all(lax.all_to_all(sent_grads.reshape(n_expert, capacity, n_gr...  25.9 us
    all_gather x1, waiting for transfers between devices, local(): shard_rows = lax.all_gather(hidden_share, 'dp', axis=0, tiled=True)  20 us
    all_to_all x1, waiting for transfers between devices, local(): lax.all_to_all(lax.all_to_all(input_grads.reshape(n_expert, capacity, n_g...  16.3 us
  transfers between devices with their start and end apart: 13, of which 11 were waited for; matrix products, arithmetic and copies ran while one was open for 14% of the time, Pallas kernels for 0%

commit v1 on v0

v1 whole, which is shorter than its diff:
```python
import functools

import jax
import jax.numpy as jnp
from jax import lax
from jax.experimental import pallas as pl
from jax.experimental.pallas import tpu as pltpu
from jax.sharding import PartitionSpec as P

MESH = pl.DeviceIdType.MESH
BF = jnp.bfloat16
F32 = jnp.float32

NZ, NY, NX, NC = 8, 4, 4, 2
CAP = 5
PAIRS = ((0, 1), (7, 2), (6, 3), (5, 4))
POS = {k: 2 * s + i for s, pair in enumerate(PAIRS) for i, k in enumerate(pair)}
HALF = 512


def dot(a, b, ca, cb):
    return lax.dot_general(a, b, (((ca,), (cb,)), ((), ())), preferred_element_type=F32)


class Sems:
    def __init__(self, send, recv):
        self.send, self.recv, self.used, self.started = send, recv, 0, []

    def copy(self, src, dst, device):
        i = self.used
        self.used += 1
        cp = pltpu.make_async_remote_copy(
            src, dst, self.send.at[i], self.recv.at[i], device_id=device, device_id_type=MESH
        )
        cp.start()
        self.started.append(cp)
        return cp


def kernel(
    tok, go, meta, wu_h, wd_h,
    gt, gg, gu_h, gd_h,
    ag_t, ag_g, low, sel, gsel, st_t, st_g, rows_t, rows_g, wu, wd,
    own, cs, cr, rs_s, rs_r, pre_sh, gdot, hid, slp,
    st_r, ret, part, zs, zr, fin, fr, gst,
    sems_s, sems_r, sems_l,
):
    e, d = lax.axis_index("expert"), lax.axis_index("dp")
    z, y, x, c = e // NY, e % NY, d // NC, d % NC
    n_dp = NX * NC
    T, D = tok.shape
    F, FF = wu.shape
    G = T * n_dp
    SG = CAP * n_dp
    CH = 2 * SG
    RP = NY * CH
    TM = ag_t.shape[2]

    def zdev(o):
        return (((z + o + NZ) % NZ) * NY + y, d)

    def ydev(o):
        return (z * NY + (y + o + NY) % NY, d)

    def xdev(o):
        return (e, ((x + o) % NX) * NC + c)

    core = (e, x * NC + (1 - c))

    def dpdev(o):
        return (e, (d + o) % n_dp)

    bar = pltpu.get_barrier_semaphore()
    peers = [dpdev(o) for o in range(1, n_dp)] + [zdev(1), zdev(-1)] + [ydev(o) for o in range(1, NY)]
    for p in peers:
        pl.semaphore_signal(bar, inc=1, device_id=p, device_id_type=MESH)
    load_u = pltpu.make_async_copy(wu_h, wu, sems_l.at[0])
    load_d = pltpu.make_async_copy(wd_h, wd, sems_l.at[1])
    load_u.start()
    load_d.start()
    pl.semaphore_wait(bar, len(peers))
    S = Sems(sems_s, sems_r)

    my_rows = pl.ds(pl.multiple_of(d * T, T), T)
    in_t, in_g = [], []
    for o in range(1, n_dp):
        cols = pl.ds(pl.multiple_of(((d + o) % n_dp) * F, 128), F)
        in_t.append(S.copy(meta, ag_t.at[0, my_rows, pl.ds(F, 128)], dpdev(o)))
        in_t.append(S.copy(tok.at[:, cols], ag_t.at[0, my_rows, pl.ds(0, F)], dpdev(o)))
    for o in range(1, n_dp):
        cols = pl.ds(pl.multiple_of(((d + o) % n_dp) * F, 128), F)
        in_g.append(S.copy(go.at[:, cols], ag_g.at[0, my_rows], dpdev(o)))
    mine = pl.ds(pl.multiple_of(d * F, 128), F)
    loc = [
        pltpu.make_async_copy(meta, ag_t.at[0, my_rows, pl.ds(F, 128)], sems_l.at[2]),
        pltpu.make_async_copy(tok.at[:, mine], ag_t.at[0, my_rows, pl.ds(0, F)], sems_l.at[3]),
        pltpu.make_async_copy(go.at[:, mine], ag_g.at[0, my_rows], sems_l.at[4]),
    ]
    for cp in loc:
        cp.start()
    ri = lax.broadcasted_iota(jnp.int32, (2 * G, 2 * G), 0)
    ci = lax.broadcasted_iota(jnp.int32, (2 * G, 2 * G), 1)
    same = (ri >> 4) == (ci >> 4)
    low[...] = jnp.where(same & (ci < ri), 1.0, 0.0).astype(BF)

    def forward(ag, h):
        up, down = h, (NZ - h) % NZ
        width = ag.shape[2]
        if h == 3:
            a, b = pl.ds(0, HALF), pl.ds(HALF, width - HALF)
            return [
                S.copy(ag.at[POS[up], :, a], ag.at[POS[4], :, a], zdev(1)),
                S.copy(ag.at[POS[down], :, b], ag.at[POS[4], :, b], zdev(-1)),
            ]
        return [
            S.copy(ag.at[POS[up]], ag.at[POS[up + 1]], zdev(1)),
            S.copy(ag.at[POS[down]], ag.at[POS[(down + 7) % NZ]], zdev(-1)),
        ]

    def select(s):
        m = ag_t[2 * s : 2 * s + 2, :, F : F + 128].reshape(2 * G, 128).astype(F32)
        lane = lax.broadcasted_iota(jnp.int32, (1, RP), 1)
        jj = sum(jnp.where(lane >= CH * i, 1, 0) for i in range(1, NY))
        q = lane - CH * jj
        blk = jnp.where(q >= SG, 1, 0)
        slot = q - SG * blk
        yy = y + jj
        yy = jnp.where(yy >= NY, yy - NY, yy)
        expert = (z * NY + yy).astype(F32)
        row = lax.broadcasted_iota(jnp.int32, (2 * G, 1), 0)
        base = CAP * ((row & (G - 1)) >> 4)
        want = jnp.where(
            jnp.where(row >= G, 1, 0) == blk, slot - base, -1
        ).astype(F32)
        hot = jnp.zeros((2 * G, RP), F32)
        gate = jnp.zeros((2 * G, RP), F32)
        for k in range(8):
            hit = m[:, k : k + 1] == expert
            hot = jnp.where(hit, 1.0, hot)
            gate = jnp.where(hit, m[:, 8 + k : 9 + k], gate)
        rank = dot(low[...], hot.astype(BF), 1, 0)
        hot = jnp.where(rank == want, hot, 0.0)
        sel[s] = hot.astype(BF)
        gsel[s] = (hot * gate).astype(BF)

    def dispatch(s, matrix, ag, stage, rows):
        block = ag[2 * s : 2 * s + 2, :, 0:F].reshape(2 * G, F)
        out = dot(matrix[s], block, 0, 0).astype(BF).reshape(NY, CH, F)
        cps = []
        for j in range(1, NY):
            stage[s * 3 + j - 1] = out[j]
            cps.append(S.copy(stage.at[s * 3 + j - 1], rows.at[s * NY + j], ydev(j)))
        rows[s * NY] = out[0]
        return cps

    y_in = {}
    core_in, rs_in, ag_in, full_in = {}, {}, {}, {}

    def product(kind, pair):
        if kind == 0:
            a = rows_t[pl.ds(pair * NY, NY)].reshape(RP, F)
            return dot(a, wu[...], 1, 0)
        a = rows_g[pl.ds(pair * NY, NY)].reshape(RP, F)
        return dot(a, wd[...], 1, 1)

    def e1(ss, kind):
        for s in (2 * ss, 2 * ss + 1):
            for cp in y_in[s, kind]:
                cp.wait_recv()
        i = 2 * ss + kind
        cs[i] = product(kind, 2 * ss + 1 - c).astype(BF)
        core_in[ss, kind] = S.copy(cs.at[i], cr.at[i], core)
        own[kind] = product(kind, 2 * ss + c)

    def e2(ss, kind):
        i = 2 * ss + kind
        core_in[ss, kind].wait_recv()
        total = own[kind] + cr[i].astype(F32)
        rs_s[pl.ds(i * NX, NX)] = total.astype(BF).reshape(NX, CH, FF)
        rs_in[ss, kind] = [
            S.copy(rs_s.at[i * NX + (x + o) % NX], rs_r.at[i * 3 + o - 1], xdev(o))
            for o in range(1, NX)
        ]

    def spread(ss, kind, ref):
        at = (2 * ss + c) * NY + x
        ag_in[ss, kind] = [S.copy(ref.at[at], ref.at[at], xdev(o)) for o in range(1, NX)]

    def e3(ss, kind):
        i = 2 * ss + kind
        for cp in rs_in[ss, kind]:
            cp.wait_recv()
        share = rs_s[i * NX + x].astype(F32)
        for o in range(3):
            share = share + rs_r[i * 3 + o].astype(F32)
        at = (2 * ss + c) * NY + x
        if kind == 0:
            pre_sh[ss] = share
            hid[at] = (share / (1.0 + jnp.exp(-share))).astype(BF)
        else:
            pre = pre_sh[ss]
            sig = 1.0 / (1.0 + jnp.exp(-pre))
            slp[at] = (share * (sig * (1.0 + pre * (1.0 - sig)))).astype(BF)
            spread(ss, 1, slp)
            gdot[ss] = jnp.broadcast_to(
                jnp.sum(hid[at].astype(F32) * share, axis=1, keepdims=True), (CH, 128)
            )

    def e4(ss, kind, ref):
        for cp in ag_in[ss, kind]:
            cp.wait_recv()
        part_of = pl.ds((2 * ss + c) * NY, NY)
        full_in[ss, kind] = S.copy(ref.at[part_of], ref.at[part_of], core)

    def e5(ss, kind):
        full_in[ss, kind].wait_recv()

    r_in = {}

    def r1(s):
        a = slp[NY * s : NY * s + NY].reshape(RP, FF)
        out = dot(a, wu[...], 1, 1).astype(BF).reshape(NY, CH, F)
        lane = lax.broadcasted_iota(jnp.int32, (CH, 128), 1)
        r_in[s] = []
        for j in [1, 2, 3, 0]:
            here = jnp.where((c == s % 2) & (x == j), 1.0, 0.0)
            gates = jnp.where(lane == e, gdot[s // 2] * here, 0.0).astype(BF)
            if j == 0:
                ret[s * NY, :, 0:F] = out[0]
                ret[s * NY, :, F : F + 128] = gates
            else:
                st_r[s * 3 + j - 1, :, 0:F] = out[j]
                st_r[s * 3 + j - 1, :, F : F + 128] = gates
                r_in[s].append(S.copy(st_r.at[s * 3 + j - 1], ret.at[s * NY + j], ydev(-j)))

    def r2(s):
        for cp in r_in[s]:
            cp.wait_recv()
        out = dot(sel[s], ret[NY * s : NY * s + NY].reshape(RP, TM), 1, 0)
        part[2 * s : 2 * s + 2] = out.reshape(2, G, TM)

    z_in = {}

    def zsend(k, to, o, value):
        zs[k] = value.astype(BF)
        z_in[to] = S.copy(zs.at[k], zr.at[to], zdev(o))

    for cp in loc:
        cp.wait()
    for cp in in_t:
        cp.wait_recv()
    hop_t = forward(ag_t, 0)
    for cp in in_g:
        cp.wait_recv()
    hop_g = forward(ag_g, 0)
    load_u.wait()
    load_d.wait()
    for h in range(1, 5):
        s = h - 1
        for cp in hop_t:
            cp.wait_recv()
        if h < 4:
            hop_t = forward(ag_t, h)
        select(s)
        y_in[s, 0] = dispatch(s, sel, ag_t, st_t, rows_t)
        for cp in hop_g:
            cp.wait_recv()
        if h < 4:
            hop_g = forward(ag_g, h)
        y_in[s, 1] = dispatch(s, gsel, ag_g, st_g, rows_g)
        if h == 3:
            e1(0, 0)
        if h == 4:
            e2(0, 0)
            e1(0, 1)
    e2(0, 1)
    e3(0, 0)
    e1(1, 0)
    e3(0, 1)
    e2(1, 0)
    e4(0, 1, slp)
    e1(1, 1)
    e3(1, 0)
    e2(1, 1)
    e5(0, 1)
    r1(1)
    r1(0)
    e3(1, 1)
    e4(1, 1, slp)
    spread(0, 0, hid)
    spread(1, 0, hid)
    e5(1, 1)
    r1(3)
    r1(2)
    e4(0, 0, hid)
    e4(1, 0, hid)

    outs = []

    def weight_grads(lhs, rhs, width, target, base):
        for i in range(0, lhs.shape[2], width):
            n = len(outs)
            a = lhs[:, :, i : i + width].reshape(4 * RP, width)
            b = rhs[...].reshape(4 * RP, rhs.shape[2])
            cols = rhs.shape[2]
            if n >= 2:
                outs[n - 2].wait()
            gst[n % 2, 0:width, 0:cols] = dot(a, b, 0, 0).astype(BF)
            cp = pltpu.make_async_copy(
                gst.at[n % 2, pl.ds(0, width), pl.ds(0, cols)],
                target.at[pl.ds(i, width)],
                sems_l.at[base + n % 2],
            )
            cp.start()
            outs.append(cp)

    r2(1)
    r2(0)
    weight_grads(rows_t, slp, 128, gu_h, 5)
    r2(3)
    zs[4] = part[POS[4]].astype(BF)
    lo, hi = pl.ds(0, HALF), pl.ds(HALF, TM - HALF)
    z_in[3] = S.copy(zs.at[4, :, lo], zr.at[3, :, lo], zdev(-1))
    z_in[5] = S.copy(zs.at[4, :, hi], zr.at[5, :, hi], zdev(1))
    r2(2)
    z_in[3].wait_recv()
    p3 = part[POS[3]]
    zs[3, :, 0:HALF] = (p3[:, 0:HALF] + zr[3, :, 0:HALF].astype(F32)).astype(BF)
    zs[3, :, HALF:TM] = p3[:, HALF:TM].astype(BF)
    z_in[2] = S.copy(zs.at[3], zr.at[2], zdev(-1))
    z_in[5].wait_recv()
    p5 = part[POS[5]]
    zs[5, :, 0:HALF] = p5[:, 0:HALF].astype(BF)
    zs[5, :, HALF:TM] = (p5[:, HALF:TM] + zr[5, :, HALF:TM].astype(F32)).astype(BF)
    z_in[6] = S.copy(zs.at[5], zr.at[6], zdev(1))
    e5(0, 0)
    e5(1, 0)
    weight_grads(hid, rows_g, 256, gd_h, 5)
    for down, up in ((2, 6), (1, 7)):
        z_in[down].wait_recv()
        zsend(down, down - 1, -1, part[POS[down]] + zr[down].astype(F32))
        z_in[up].wait_recv()
        zsend(up, up + 1, 1, part[POS[up]] + zr[up].astype(F32))
    z_in[0].wait_recv()
    z_in[8].wait_recv()
    fin[...] = (part[POS[0]] + zr[0].astype(F32) + zr[8].astype(F32)).astype(BF).reshape(n_dp, T, TM)

    last = [S.copy(fin.at[(d + o) % n_dp], fr.at[d], dpdev(o)) for o in range(1, n_dp)]
    keep = pltpu.make_async_copy(fin.at[d], fr.at[d], sems_l.at[7])
    keep.start()
    keep.wait()
    for cp in last:
        cp.wait_recv()
    lanes = jnp.zeros((T, 128), F32)
    for i in range(n_dp):
        gt[:, i * F : (i + 1) * F] = fr[i, :, 0:F]
        lanes = lanes + fr[i, :, F : F + 128].astype(F32)
    m = meta[...].astype(F32)
    lane = lax.broadcasted_iota(jnp.int32, (T, 128), 1)
    lane_f = lane.astype(F32)
    res = jnp.zeros((T, 128), F32)
    for k in range(8):
        v = jnp.sum(jnp.where(m[:, k : k + 1] == lane_f, lanes, 0.0), axis=1, keepdims=True)
        res = jnp.where(lane == k, v / m[:, 8 + k : 9 + k], res)
    gg[...] = res
    for cp in outs[-2:]:
        cp.wait()
    for cp in S.started:
        cp.wait_send()


def local(tokens, grad_out, routes, gates, w_up, w_down):
    T, D = tokens.shape
    _, F, FF = w_up.shape
    n_dp = NX * NC
    G, CH = T * n_dp, 2 * CAP * n_dp
    RP = NY * CH
    TM = F + 128
    meta = jnp.concatenate(
        [routes.astype(BF), gates, jnp.zeros((T, 128 - 16), BF)], axis=1
    )
    vm = pl.BlockSpec(memory_space=pltpu.VMEM)
    hbm = pl.BlockSpec(memory_space=pl.ANY)
    V = pltpu.VMEM
    gt, gg, gu, gd = pl.pallas_call(
        kernel,
        out_shape=(
            jax.ShapeDtypeStruct((T, D), BF),
            jax.ShapeDtypeStruct((T, 128), F32),
            jax.ShapeDtypeStruct((F, FF), BF),
            jax.ShapeDtypeStruct((FF, F), BF),
        ),
        in_specs=[vm, vm, vm, hbm, hbm],
        out_specs=(vm, vm, hbm, hbm),
        scratch_shapes=[
            V((NZ, G, TM), BF),
            V((NZ, G, F), BF),
            V((2 * G, 2 * G), BF),
            V((4, 2 * G, RP), BF),
            V((4, 2 * G, RP), BF),
            V((12, CH, F), BF),
            V((12, CH, F), BF),
            V((16, CH, F), BF),
            V((16, CH, F), BF),
            V((F, FF), BF),
            V((FF, F), BF),
            V((2, RP, FF), F32),
            V((4, RP, FF), BF),
            V((4, RP, FF), BF),
            V((16, CH, FF), BF),
            V((12, CH, FF), BF),
            V((2, CH, FF), F32),
            V((2, CH, 128), F32),
            V((16, CH, FF), BF),
            V((16, CH, FF), BF),
            V((12, CH, TM), BF),
            V((16, CH, TM), BF),
            V((NZ, G, TM), F32),
            V((NZ, G, TM), BF),
            V((NZ + 1, G, TM), BF),
            V((n_dp, T, TM), BF),
            V((n_dp, T, TM), BF),
            V((2, 256, FF), BF),
            pltpu.SemaphoreType.DMA((140,)),
            pltpu.SemaphoreType.DMA((140,)),
            pltpu.SemaphoreType.DMA((8,)),
        ],
        compiler_params=pltpu.CompilerParams(
            collective_id=0, has_side_effects=True, vmem_limit_bytes=63 * 1024 * 1024
        ),
    )(tokens, grad_out, meta, w_up[0], w_down[0])
    return gt, gg[:, : routes.shape[1]], gu[None], gd[None]


def solution(mesh):
    rows = P(("expert", "dp"), None)
    return jax.shard_map(
        local,
        mesh=mesh,
        in_specs=(rows, rows, rows, rows, P("expert", "dp", None), P("expert", None, "dp")),
        out_specs=(rows, rows, P("expert", "dp", None), P("expert", None, "dp")),
        check_vma=False,
    )
```

time: 454 us -> 175 us (0.39)
  waiting for transfers between devices: 264 us -> 0 us
  Pallas kernels: 0 us -> 163 us
  starting transfers between devices: 66.6 us -> 0 us
  matrix products: 35.8 us -> 0 us
  blocking collectives: 33.9 us -> 0 us
  local copies, waits for them, and re-layouts: 28.9 us -> 8.16 us
  between operations: 14 us -> 0.65 us
  other arithmetic: 9.81 us -> 1.36 us
    all_to_all x9 -> x0, waiting for transfers between devices: 198 us -> none  [the longest x1 51.7 us: local(): lax.all_to_all(input_grads.reshape(n_expert, capacity, n_group, feat_widt...]
    pallas_call x0 -> x1, Pallas kernels: none -> 163 us  [local(): pl.pallas_call(kernel, out_shape=(jax.ShapeDtypeStruct((T, D), BF), jax.S...]
    all_to_all x9 -> x0, starting transfers between devices: 66.2 us -> none  [the longest x1 12 us: local(): lax.all_to_all(gate_block, 'expert', split_axis=0, concat_axis=0, tiled=T...]
    dot_general x11 -> x0, matrix products: 35.8 us -> none  [the longest x1 6.39 us: local(): lax.dot_general(in_rows, shard_rows, contract_rows, preferred_element_typ...]
    all_gather x2 -> x0, waiting for transfers between devices: 34.9 us -> none  [the longest x1 20 us: local(): shard_rows = lax.all_gather(hidden_share, 'dp', axis=0, tiled=True)]
    all_to_all x1 -> x0, blocking collectives: 33.9 us -> none  [local(): lax.all_to_all(lax.all_to_all(sent_inputs.reshape(n_expert, capacity, n_g...]
    reduce_scatter x2 -> x0, waiting for transfers between devices: 30.6 us -> none  [the longest x1 30.5 us: local(): lax.psum_scatter(jnp.dot(in_rows, up_weight, preferred_element_type=jnp.f...]
    all_to_all x7 -> x0, local copies, waits for them, and re-layouts: 13.2 us -> none  [the longest x1 3.36 us: local(): lax.all_to_all(input_grads.reshape(n_expert, capacity, n_group, feat_widt...]
  transfers between devices with their start and end apart: 13 -> 0, of which waited for: 11 -> 0; matrix products, arithmetic and copies ran while one was open for 14% -> 0% of each run, Pallas kernels for 0% -> 0%
where the time goes in v1:
time: 175 us; the launch traced here: 173 us
  Pallas kernels  163 us (93%)
  local copies, waits for them, and re-layouts  8.16 us (5%)
    pallas_call x1, Pallas kernels, local(): pl.pallas_call(kernel, out_shape=(jax.ShapeDtypeStruct((T, D), BF), jax.S...  163 us
    unnamed x7, local copies, waits for them, and re-layouts  7.99 us

profile of v1, /device:TPU:1, one launch (start us, length us, event | category | flops | bytes accessed | tf_op | source)
XLA Modules:
  0.0 172.9 jit_solution(2232570497478863204)
XLA Ops:
  0.6 0.1 pad.2.clone
  0.7 0.7 convert_element_type.3
  1.4 0.1 copy.13
  1.5 0.8 copy.14
  2.3 0.7 maximum_maximum_fusion.meta
  2.9 162.8 %shard_map.93 = (bf16[16,7168]{1,0:T(8,128)(2,1)}, f32[16,128]{1,0:T(8,128)}, bf16[896,1024]{1,0:T(8,128)(2,1)}, bf16[1024,896]{1,0:T(8,128)(2,1)}) custom-call(bf16[16,7168]{1,0:T(8,128)(2,1)} %tok.1, bf16[16,7168]{1,0:T(8,128)(2,1)} %go.1, bf16[16,128]{1,0:T(8,128)(2,1)} %maximum_maximum_fusion.meta, bf16[896,1024]{1,0:T(8,128)(2,1)} %bitcast.5, ...), custom_call_target="tpu_custom_call" | custom-call | tf_op jit(solution)/shard_map/pallas_call | solution.py:385
  165.7 1.4 copy.15
  167.1 1.6 copy.19
  168.7 0.0 copy-start
  168.7 3.0 %copy.20 = bf16[1,896,1024]{2,1,0:T(8,128)(2,1)} copy(bf16[1,896,1024]{2,1,0:T(8,128)(2,1)} %bitcast.8) | data formatting | bytes 3670016
  171.7 0.0 copy-done
  171.7 1.2 copy.21
  (1 shorter events, 0.0 us)
Async XLA Ops:
  168.7 3.0 %copy-start = (bf16[1024,896]{1,0:T(8,128)(2,1)S(1)}, bf16[1024,896]{1,0:T(8,128)(2,1)}, u32[]{:S(2)}) copy-start(bf16[1024,896]{1,0:T(8,128)(2,1)} %get-tuple-element.11) | copy-start | bytes 5505028

commit v2 on v1

v2 whole, which is shorter than its diff:
```python
import functools

import jax
import jax.numpy as jnp
from jax import lax
from jax.experimental import pallas as pl
from jax.experimental.pallas import tpu as pltpu
from jax.sharding import PartitionSpec as P

MESH = pl.DeviceIdType.MESH
BF = jnp.bfloat16
F32 = jnp.float32

NZ, NY, NX, NC = 8, 4, 4, 2
CAP = 5
QUADS = ((0, 1, 7, 2), (6, 3, 5, 4))
POS = {k: 4 * q + i for q, quad in enumerate(QUADS) for i, k in enumerate(quad)}
CUT = 512


def mark(n):
    pass


def dot(a, b, ca, cb):
    return lax.dot_general(a, b, (((ca,), (cb,)), ((), ())), preferred_element_type=F32)


class Sems:
    def __init__(self, send, recv):
        self.send, self.recv, self.used, self.started = send, recv, 0, []

    def copy(self, src, dst, device):
        i = self.used
        self.used += 1
        cp = pltpu.make_async_remote_copy(
            src, dst, self.send.at[i], self.recv.at[i], device_id=device, device_id_type=MESH
        )
        cp.start()
        self.started.append(cp)
        return cp


def kernel(
    tok_h, go_h, routes, gates, wu_h, wd_h,
    gt_h, gg, gu_h, gd_h,
    tok, go, meta, ag_t, ag_g, low, sel, gsel, st_t, st_g, rows_t, rows_g, wu, wd,
    own, cs, cr, rs_s, rs_r, pre_sh, gdot, hid, slp,
    st_r, ret, part, zs, zr, fin, fr, gst,
    sems_s, sems_r, sems_l,
):
    e, d = lax.axis_index("expert"), lax.axis_index("dp")
    z, y, x, c = e // NY, e % NY, d // NC, d % NC
    n_dp = NX * NC
    T, D = tok.shape
    _, F, FH = wu.shape
    B = T * n_dp // 2
    SB = CAP * n_dp // 2
    CH = 4 * SB
    RP = NY * CH
    TM = ag_t.shape[2]

    def zdev(o):
        return (((z + o + NZ) % NZ) * NY + y, d)

    def ydev(o):
        return (z * NY + (y + o + NY) % NY, d)

    def xdev(o):
        return (e, ((x + o) % NX) * NC + c)

    core = (e, x * NC + (1 - c))

    def dpdev(o):
        return (e, (d + o) % n_dp)

    bar = pltpu.get_barrier_semaphore()
    peers = [dpdev(o) for o in range(1, n_dp)] + [zdev(1), zdev(-1)] + [ydev(o) for o in range(1, NY)]
    takes = [
        pltpu.make_async_copy(tok_h, tok, sems_l.at[10]),
        pltpu.make_async_copy(go_h, go, sems_l.at[11]),
    ]
    for cp in takes:
        cp.start()
    for p in peers:
        pl.semaphore_signal(bar, inc=1, device_id=p, device_id_type=MESH)
    loads = [
        pltpu.make_async_copy(wu_h.at[:, pl.ds(h * FH, FH)], wu.at[h], sems_l.at[h]) for h in range(2)
    ] + [
        pltpu.make_async_copy(wd_h.at[pl.ds(h * FH, FH)], wd.at[h], sems_l.at[2 + h]) for h in range(2)
    ]
    for cp in loads:
        cp.start()
    k_in = lax.broadcasted_iota(jnp.int32, (8, 128), 0)
    k_out = lax.broadcasted_iota(jnp.int32, (8, 128), 1)
    meta[...] = (
        dot(routes[...].astype(F32).astype(BF), jnp.where(k_in == k_out, 1.0, 0.0).astype(BF), 0, 0)
        + dot(gates[...], jnp.where(k_in + 8 == k_out, 1.0, 0.0).astype(BF), 0, 0)
    ).astype(BF)
    for cp in takes:
        cp.wait()
    pl.semaphore_wait(bar, len(peers))
    S = Sems(sems_s, sems_r)
    mark("bar")

    my_half = (d // NY) * NZ
    my_rows = pl.ds(pl.multiple_of((d % NY) * T, T), T)
    in_t, in_g = [], []
    for o in range(1, n_dp):
        cols = pl.ds(pl.multiple_of(((d + o) % n_dp) * F, 128), F)
        in_t.append(S.copy(meta, ag_t.at[my_half, my_rows, pl.ds(F, 128)], dpdev(o)))
        in_t.append(S.copy(tok.at[:, cols], ag_t.at[my_half, my_rows, pl.ds(0, F)], dpdev(o)))
    for o in range(1, n_dp):
        cols = pl.ds(pl.multiple_of(((d + o) % n_dp) * F, 128), F)
        in_g.append(S.copy(go.at[:, cols], ag_g.at[my_half, my_rows], dpdev(o)))
    mine = pl.ds(pl.multiple_of(d * F, 128), F)
    loc = [
        pltpu.make_async_copy(meta, ag_t.at[my_half, my_rows, pl.ds(F, 128)], sems_l.at[4]),
        pltpu.make_async_copy(tok.at[:, mine], ag_t.at[my_half, my_rows, pl.ds(0, F)], sems_l.at[5]),
        pltpu.make_async_copy(go.at[:, mine], ag_g.at[my_half, my_rows], sems_l.at[6]),
    ]
    for cp in loc:
        cp.start()
    ri = lax.broadcasted_iota(jnp.int32, (4 * B, 4 * B), 0)
    ci = lax.broadcasted_iota(jnp.int32, (4 * B, 4 * B), 1)
    same = (ri >> 4) == (ci >> 4)
    low[...] = jnp.where(same & (ci < ri), 1.0, 0.0).astype(BF)

    hops = {}

    def forward(ag, kind, a, h):
        up, down, at = h, (NZ - h) % NZ, a * NZ
        width = ag.shape[2]
        if h == 3:
            lo, hi = pl.ds(0, CUT), pl.ds(CUT, width - CUT)
            hops[kind, a] = [
                S.copy(ag.at[at + POS[up], :, lo], ag.at[at + POS[4], :, lo], zdev(1)),
                S.copy(ag.at[at + POS[down], :, hi], ag.at[at + POS[4], :, hi], zdev(-1)),
            ]
        else:
            hops[kind, a] = [
                S.copy(ag.at[at + POS[up]], ag.at[at + POS[up + 1]], zdev(1)),
                S.copy(ag.at[at + POS[down]], ag.at[at + POS[(down + 7) % NZ]], zdev(-1)),
            ]

    def hop(a, h, kind):
        for cp in hops[kind, a]:
            cp.wait_recv()
        if h < 4:
            forward((ag_t, ag_g)[kind], kind, a, h)

    def select(u):
        m = ag_t[4 * u : 4 * u + 4, :, F : F + 128].reshape(4 * B, 128).astype(F32)
        lane = lax.broadcasted_iota(jnp.int32, (1, RP), 1)
        jj = sum(jnp.where(lane >= CH * i, 1, 0) for i in range(1, NY))
        q = lane - CH * jj
        blk = sum(jnp.where(q >= SB * i, 1, 0) for i in range(1, 4))
        slot = q - SB * blk
        yy = y + jj
        yy = jnp.where(yy >= NY, yy - NY, yy)
        expert = (z * NY + yy).astype(F32)
        row = lax.broadcasted_iota(jnp.int32, (4 * B, 1), 0)
        base = CAP * ((row & (B - 1)) >> 4)
        row_blk = sum(jnp.where(row >= B * i, 1, 0) for i in range(1, 4))
        want = jnp.where(row_blk == blk, slot - base, -1).astype(F32)
        hot = jnp.zeros((4 * B, RP), F32)
        gate = jnp.zeros((4 * B, RP), F32)
        for k in range(8):
            hit = m[:, k : k + 1] == expert
            hot = jnp.where(hit, 1.0, hot)
            gate = jnp.where(hit, m[:, 8 + k : 9 + k], gate)
        rank = dot(low[...], hot.astype(BF), 1, 0)
        hot = jnp.where(rank == want, hot, 0.0)
        sel[u] = hot.astype(BF)
        gsel[u] = (hot * gate).astype(BF)

    y_in = {}
    core_in, rs_in, ag_in, full_in = {}, {}, {}, {}

    def dispatch(u, kind):
        if kind == 0:
            select(u)
        matrix, ag, stage, rows = ((sel, ag_t, st_t, rows_t), (gsel, ag_g, st_g, rows_g))[kind]
        block = ag[4 * u : 4 * u + 4, :, 0:F].reshape(4 * B, F)
        out = dot(matrix[u], block, 0, 0).astype(BF).reshape(NY, CH, F)
        y_in[u, kind] = []
        for j in range(1, NY):
            stage[u * 3 + j - 1] = out[j]
            y_in[u, kind].append(S.copy(stage.at[u * 3 + j - 1], rows.at[u * NY + j], ydev(j)))
        rows[u * NY] = out[0]

    def e1(u, kind):
        for cp in y_in[u, kind]:
            cp.wait_recv()
        i = 2 * u + kind
        a = (rows_t, rows_g)[kind][u * NY : u * NY + NY].reshape(RP, F)
        w, dim = ((wu, 0), (wd, 1))[kind]
        cs[i] = dot(a, w[1 - c], 1, dim).astype(BF)
        core_in[u, kind] = S.copy(cs.at[i], cr.at[i], core)
        own[i % 4] = dot(a, w[c], 1, dim)

    def e2(u, kind):
        i = 2 * u + kind
        core_in[u, kind].wait_recv()
        total = own[i % 4] + cr[i].astype(F32)
        rs_s[i * NX : i * NX + NX] = total.astype(BF).reshape(NX, CH, FH)
        rs_in[u, kind] = [
            S.copy(rs_s.at[i * NX + (x + o) % NX], rs_r.at[i * 3 + o - 1], xdev(o))
            for o in range(1, NX)
        ]

    def spread(u, kind):
        ref = (hid, slp)[kind]
        at = u * NY + x
        ag_in[u, kind] = [S.copy(ref.at[c, at], ref.at[c, at], xdev(o)) for o in range(1, NX)]

    def e3(u, kind):
        i = 2 * u + kind
        for cp in rs_in[u, kind]:
            cp.wait_recv()
        share = rs_s[i * NX + x].astype(F32)
        for o in range(3):
            share = share + rs_r[i * 3 + o].astype(F32)
        at = u * NY + x
        if kind == 0:
            pre_sh[u] = share
            hid[c, at] = (share / (1.0 + jnp.exp(-share))).astype(BF)
        else:
            pre = pre_sh[u]
            sig = 1.0 / (1.0 + jnp.exp(-pre))
            slp[c, at] = (share * (sig * (1.0 + pre * (1.0 - sig)))).astype(BF)
            spread(u, 1)
            gdot[u] = jnp.broadcast_to(
                jnp.sum(hid[c, at].astype(F32) * share, axis=1, keepdims=True), (CH, 128)
            )

    def e4(u, kind):
        ref = (hid, slp)[kind]
        for cp in ag_in[u, kind]:
            cp.wait_recv()
        part_of = pl.ds(u * NY, NY)
        full_in[u, kind] = S.copy(ref.at[c, part_of], ref.at[c, part_of], core)

    def e5(u, kind):
        full_in[u, kind].wait_recv()

    r_in = {}

    def r1(u):
        rows = slice(NY * u, NY * u + NY)
        out = dot(slp[0, rows].reshape(RP, FH), wu[0], 1, 1)
        out = out + dot(slp[1, rows].reshape(RP, FH), wu[1], 1, 1)
        out = out.astype(BF).reshape(NY, CH, F)
        lane = lax.broadcasted_iota(jnp.int32, (CH, 128), 1)
        r_in[u] = []
        for j in [1, 2, 3, 0]:
            here = jnp.where(x == j, 1.0, 0.0)
            dots = jnp.where(lane == e, gdot[u] * here, 0.0).astype(BF)
            if j == 0:
                ret[u * NY, :, 0:F] = out[0]
                ret[u * NY, :, F : F + 128] = dots
            else:
                st_r[u * 3 + j - 1, :, 0:F] = out[j]
                st_r[u * 3 + j - 1, :, F : F + 128] = dots
                r_in[u].append(S.copy(st_r.at[u * 3 + j - 1], ret.at[u * NY + j], ydev(-j)))

    def r2(u):
        for cp in r_in[u]:
            cp.wait_recv()
        out = dot(sel[u], ret[NY * u : NY * u + NY].reshape(RP, TM), 1, 0)
        part[4 * u : 4 * u + 4] = out.reshape(4, B, TM)

    z_in = {}

    def chain(a, step):
        p, s_at, r_at = a * NZ, a * NZ, a * (NZ + 1)
        lo, hi = pl.ds(0, CUT), pl.ds(CUT, TM - CUT)
        if step == 1:
            zs[s_at + 4] = part[p + POS[4]].astype(BF)
            z_in[a, 3] = S.copy(zs.at[s_at + 4, :, lo], zr.at[r_at + 3, :, lo], zdev(-1))
            z_in[a, 5] = S.copy(zs.at[s_at + 4, :, hi], zr.at[r_at + 5, :, hi], zdev(1))
            return
        if step == 5:
            z_in[a, 0].wait_recv()
            z_in[a, 8].wait_recv()
            total = part[p + POS[0]] + zr[r_at].astype(F32) + zr[r_at + 8].astype(F32)
            fin[a * NY : a * NY + NY] = total.astype(BF).reshape(NY, T, TM)
            return
        down, up = 5 - step, 3 + step
        z_in[a, down].wait_recv()
        if step == 2:
            mid = part[p + POS[3]]
            zs[s_at + 3, :, 0:CUT] = (mid[:, 0:CUT] + zr[r_at + 3, :, 0:CUT].astype(F32)).astype(BF)
            zs[s_at + 3, :, CUT:TM] = mid[:, CUT:TM].astype(BF)
        else:
            zs[s_at + down] = (part[p + POS[down]] + zr[r_at + down].astype(F32)).astype(BF)
        z_in[a, down - 1] = S.copy(zs.at[s_at + down], zr.at[r_at + down - 1], zdev(-1))
        z_in[a, up].wait_recv()
        if step == 2:
            mid = part[p + POS[5]]
            zs[s_at + 5, :, 0:CUT] = mid[:, 0:CUT].astype(BF)
            zs[s_at + 5, :, CUT:TM] = (mid[:, CUT:TM] + zr[r_at + 5, :, CUT:TM].astype(F32)).astype(BF)
        else:
            zs[s_at + up] = (part[p + POS[up]] + zr[r_at + up].astype(F32)).astype(BF)
        z_in[a, up + 1] = S.copy(zs.at[s_at + up], zr.at[r_at + up + 1], zdev(1))

    outs = []

    def weight_rows(kind, h, i, width):
        n = len(outs)
        if n >= 2:
            outs[n - 2].wait()
        lhs = (rows_t[:, :, i : i + width] if kind == 0 else hid[h, :, :, i : i + width])
        lhs = lhs.reshape(4 * RP, width)
        if kind == 0:
            for g in range(2):
                gst[n % 2, 0:width, g * FH : g * FH + FH] = dot(
                    lhs, slp[g].reshape(4 * RP, FH), 0, 0
                ).astype(BF)
            cp = pltpu.make_async_copy(
                gst.at[n % 2, pl.ds(0, width)], gu_h.at[pl.ds(i, width)], sems_l.at[8 + n % 2]
            )
        else:
            gst[n % 2, 0:width, 0:F] = dot(lhs, rows_g[...].reshape(4 * RP, F), 0, 0).astype(BF)
            cp = pltpu.make_async_copy(
                gst.at[n % 2, pl.ds(0, width), pl.ds(0, F)],
                gd_h.at[pl.ds(h * FH + i, width)],
                sems_l.at[8 + n % 2],
            )
        cp.start()
        outs.append(cp)

    for cp in loc:
        cp.wait()
    for cp in in_t:
        cp.wait_recv()
    forward(ag_t, 0, 0, 0)
    for cp in in_g:
        cp.wait_recv()
    forward(ag_g, 1, 0, 0)
    mark("z0")
    hop(0, 1, 0)
    hop(0, 1, 1)
    hop(0, 2, 0)
    dispatch(0, 0)
    hop(0, 2, 1)
    forward(ag_t, 0, 1, 0)
    dispatch(0, 1)
    forward(ag_g, 1, 1, 0)
    mark("d0")
    hop(0, 3, 0)
    hop(0, 3, 1)
    for cp in loads:
        cp.wait()
    hop(0, 4, 0)
    dispatch(1, 0)
    hop(0, 4, 1)
    dispatch(1, 1)
    mark("d1")
    e1(0, 0)
    hop(1, 1, 0)
    hop(1, 1, 1)
    e2(0, 0)
    e1(0, 1)
    hop(1, 2, 0)
    dispatch(2, 0)
    hop(1, 2, 1)
    dispatch(2, 1)
    mark("d2")
    e2(0, 1)
    e3(0, 0)
    spread(0, 0)
    e1(1, 0)
    hop(1, 3, 0)
    hop(1, 3, 1)
    e2(1, 0)
    e3(0, 1)
    hop(1, 4, 0)
    dispatch(3, 0)
    hop(1, 4, 1)
    dispatch(3, 1)
    mark("d3")
    e1(1, 1)
    e3(1, 0)
    e2(1, 1)
    e4(0, 1)
    e1(2, 0)
    e5(0, 1)
    e2(2, 0)
    e3(1, 1)
    mark("e3_11")
    e1(2, 1)
    e3(2, 0)
    e4(1, 1)
    e2(2, 1)
    e5(1, 1)
    e1(3, 0)
    e3(2, 1)
    e2(3, 0)
    mark("e2_30")
    r1(1)
    r1(0)
    mark("r1_0")
    e1(3, 1)
    e4(2, 1)
    e3(3, 0)
    e2(3, 1)
    mark("e2_31")
    e5(2, 1)
    e3(3, 1)
    r2(1)
    chain(0, 1)
    e4(3, 1)
    spread(1, 0)
    spread(2, 0)
    spread(3, 0)
    mark("e4_31")
    chain(0, 2)
    e5(3, 1)
    r1(3)
    r1(2)
    mark("r1_2")
    r2(0)
    chain(0, 3)
    weight_rows(0, 0, 0, 256)
    chain(0, 4)
    weight_rows(0, 0, 256, 256)
    e4(0, 0)
    chain(0, 5)
    mark("chain0")
    r2(3)
    chain(1, 1)
    for u in (1, 2, 3):
        e4(u, 0)
    mark("r2_3")
    weight_rows(0, 0, 512, 256)
    weight_rows(0, 0, 768, 128)
    chain(1, 2)
    mark("c2")
    for u in range(4):
        e5(u, 0)
    weight_rows(1, 0, 0, 256)
    r2(2)
    chain(1, 3)
    weight_rows(1, 0, 256, 256)
    weight_rows(1, 1, 0, 256)
    chain(1, 4)
    weight_rows(1, 1, 256, 256)
    mark("c4")
    chain(1, 5)
    mark("c5")

    last = [S.copy(fin.at[(d + o) % n_dp], fr.at[d], dpdev(o)) for o in range(1, n_dp)]
    keep = pltpu.make_async_copy(fin.at[d], fr.at[d], sems_l.at[7])
    keep.start()
    m = meta[...].astype(F32)
    lane = lax.broadcasted_iota(jnp.int32, (T, 128), 1).astype(F32)
    keep.wait()
    for cp in last:
        cp.wait_recv()
    stores = [
        pltpu.make_async_copy(
            fr.at[i, :, pl.ds(0, F)], gt_h.at[:, pl.ds(i * F, F)], sems_l.at[12 + i]
        )
        for i in range(n_dp)
    ]
    for cp in stores:
        cp.start()
    lanes = jnp.zeros((T, 128), F32)
    for i in range(n_dp):
        lanes = lanes + fr[i, :, F : F + 128].astype(F32)
    res = jnp.zeros((T, 128), F32)
    for k in range(8):
        v = jnp.sum(jnp.where(m[:, k : k + 1] == lane, lanes, 0.0), axis=1, keepdims=True)
        res = jnp.where(lane == k, v / m[:, 8 + k : 9 + k], res)
    gg[...] = lax.transpose(res, (1, 0))[0:8]
    for cp in outs[-2:] + stores:
        cp.wait()
    for cp in S.started:
        cp.wait_send()


def finish(*refs):
    n = (len(refs) - 2) // 3
    stage, (sin, sout) = refs[2 * n : 3 * n], refs[3 * n :]
    cps = []
    for src, mid, dst in zip(refs[:n], stage, refs[n : 2 * n]):
        rows = src.shape[0]
        step = rows // 4 if rows > 16 else rows
        for i in range(0, rows, step):
            at, k = pl.ds(i, step), len(cps)
            take = pltpu.make_async_copy(src.at[at], mid.at[at], sin.at[k])
            take.start()
            cps.append((take, pltpu.make_async_copy(mid.at[at], dst.at[at], sout.at[k])))
    for take, put in cps:
        take.wait()
        put.start()
    for take, put in cps:
        put.wait()


def local(tokens, grad_out, routes, gates, w_up, w_down):
    T, D = tokens.shape
    _, F, FF = w_up.shape
    n_dp, FH = NX * NC, FF // 2
    B, CH = T * n_dp // 2, 2 * CAP * n_dp
    RP = NY * CH
    TM = F + 128
    vm = pl.BlockSpec(memory_space=pltpu.VMEM)
    hbm = pl.BlockSpec(memory_space=pl.ANY)
    V = pltpu.VMEM
    gt, gg, gu, gd = pl.pallas_call(
        kernel,
        out_shape=(
            jax.ShapeDtypeStruct((T, D), BF),
            jax.ShapeDtypeStruct((routes.shape[1], T), F32),
            jax.ShapeDtypeStruct((F, FF), BF),
            jax.ShapeDtypeStruct((FF, F), BF),
        ),
        in_specs=[hbm, hbm, vm, vm, hbm, hbm],
        out_specs=(hbm, vm, hbm, hbm),
        scratch_shapes=[
            V((T, D), BF),
            V((T, D), BF),
            V((T, 128), BF),
            V((2 * NZ, B, TM), BF),
            V((2 * NZ, B, F), BF),
            V((4 * B, 4 * B), BF),
            V((4, 4 * B, RP), BF),
            V((4, 4 * B, RP), BF),
            V((12, CH, F), BF),
            V((12, CH, F), BF),
            V((16, CH, F), BF),
            V((16, CH, F), BF),
            V((2, F, FH), BF),
            V((2, FH, F), BF),
            V((4, RP, FH), F32),
            V((8, RP, FH), BF),
            V((8, RP, FH), BF),
            V((32, CH, FH), BF),
            V((24, CH, FH), BF),
            V((4, CH, FH), F32),
            V((4, CH, 128), F32),
            V((2, 16, CH, FH), BF),
            V((2, 16, CH, FH), BF),
            V((12, CH, TM), BF),
            V((16, CH, TM), BF),
            V((2 * NZ, B, TM), F32),
            V((2 * NZ, B, TM), BF),
            V((2 * NZ + 2, B, TM), BF),
            V((n_dp, T, TM), BF),
            V((n_dp, T, TM), BF),
            V((2, 256, FF), BF),
            pltpu.SemaphoreType.DMA((180,)),
            pltpu.SemaphoreType.DMA((180,)),
            pltpu.SemaphoreType.DMA((20,)),
        ],
        compiler_params=pltpu.CompilerParams(
            collective_id=0, has_side_effects=True, vmem_limit_bytes=63 * 1024 * 1024
        ),
    )(tokens, grad_out, routes.T, gates.T, w_up[0], w_down[0])
    made = (gt, gg, gu, gd)
    gt, gg, gu, gd = pl.pallas_call(
        finish,
        out_shape=tuple(jax.ShapeDtypeStruct(a.shape, a.dtype) for a in made),
        in_specs=[hbm] * 4,
        out_specs=(hbm,) * 4,
        scratch_shapes=[V(a.shape, a.dtype) for a in made]
        + [pltpu.SemaphoreType.DMA((16,)), pltpu.SemaphoreType.DMA((16,))],
        compiler_params=pltpu.CompilerParams(vmem_limit_bytes=63 * 1024 * 1024),
    )(*made)
    return gt, gg.T, gu[None], gd[None]


def solution(mesh):
    rows = P(("expert", "dp"), None)
    return jax.shard_map(
        local,
        mesh=mesh,
        in_specs=(rows, rows, rows, rows, P("expert", "dp", None), P("expert", None, "dp")),
        out_specs=(rows, rows, P("expert", "dp", None), P("expert", None, "dp")),
        check_vma=False,
    )
```

time: 175 us -> 152 us (0.87); the launches traced: 173 us -> 152 us
  Pallas kernels: 163 us -> 151 us
  local copies, waits for them, and re-layouts: 8.16 us -> 0 us
    pallas_call x1, Pallas kernels: 163 us -> 148 us  [local(): pl.pallas_call(kernel, out_shape=(jax.ShapeDtypeStruct((T, D), BF), jax.S...]
    unnamed x7 -> x0, local copies, waits for them, and re-layouts: 7.99 us -> none
    pallas_call x0 -> x1, Pallas kernels: none -> 3.61 us  [local(): pl.pallas_call(finish, out_shape=tuple((jax.ShapeDtypeStruct(a.shape, a.d...]
where the time goes in v2:
time: 152 us
  Pallas kernels  151 us (99%)
    pallas_call x1, Pallas kernels, local(): pl.pallas_call(kernel, out_shape=(jax.ShapeDtypeStruct((T, D), BF), jax.S...  148 us
    pallas_call x1, Pallas kernels, local(): pl.pallas_call(finish, out_shape=tuple((jax.ShapeDtypeStruct(a.shape, a.d...  3.61 us

profile of v2, /device:TPU:1, one launch (start us, length us, event | category | flops | bytes accessed | tf_op | source)
XLA Modules:
  0.0 152.1 jit_solution(10859154683245688123)
XLA Ops:
  0.6 147.6 %shard_map.93 = (bf16[16,7168]{1,0:T(8,128)(2,1)}, f32[8,16]{1,0:T(8,128)}, bf16[896,1024]{1,0:T(8,128)(2,1)}, bf16[1024,896]{1,0:T(8,128)(2,1)}) custom-call(bf16[16,7168]{1,0:T(8,128)(2,1)} %tok_h.1, bf16[16,7168]{1,0:T(8,128)(2,1)} %go_h.1, s32[8,16]{1,0:T(8,128)} %bitcast.9, bf16[8,16]{1,0:T(8,128)(2,1)} %bitcast.10, bf16[896,1024]{1,0:T(8,128)(2,1)} %bitcast.7, ...), custom_call_target="tpu_custom_call" | custom-call | tf_op jit(solution)/shard_map/pallas_call | solution.py:512
  148.3 3.6 %shard_map.94 = (bf16[16,7168]{1,0:T(8,128)(2,1)}, f32[8,16]{1,0:T(8,128)}, bf16[896,1024]{1,0:T(8,128)(2,1)}, bf16[1024,896]{1,0:T(8,128)(2,1)}) custom-call(bf16[16,7168]{1,0:T(8,128)(2,1)} %get-tuple-element.12.refs_0_, f32[8,16]{1,0:T(8,128)} %get-tuple-element.13.refs_1_, bf16[896,1024]{1,0:T(8,128)(2,1)} %get-tuple-element.14.refs_2_, ...), custom_call_target="tpu_custom_call" | custom-call | tf_op jit(solution)/shard_map/pallas_call | solution.py:563

commit v3 on v2

--- a/solution.py
+++ b/solution.py
@@ -344,12 +344,12 @@
     hop(0, 2, 0)
     dispatch(0, 0)
     hop(0, 2, 1)
-    forward(ag_t, 0, 1, 0)
     dispatch(0, 1)
-    forward(ag_g, 1, 1, 0)
     mark("d0")
     hop(0, 3, 0)
     hop(0, 3, 1)
+    forward(ag_t, 0, 1, 0)
+    forward(ag_g, 1, 1, 0)
     for cp in loads:
         cp.wait()
     hop(0, 4, 0)

time: 152 us -> 150 us (0.987)
  Pallas kernels: 151 us -> 149 us
    pallas_call x1, Pallas kernels: 148 us -> 145 us  [local(): pl.pallas_call(kernel, out_shape=(jax.ShapeDtypeStruct((T, D), BF), jax.S...]
where the time goes in v3:
time: 150 us
  Pallas kernels  149 us (99%)
    pallas_call x1, Pallas kernels, local(): pl.pallas_call(kernel, out_shape=(jax.ShapeDtypeStruct((T, D), BF), jax.S...  145 us
    pallas_call x1, Pallas kernels, local(): pl.pallas_call(finish, out_shape=tuple((jax.ShapeDtypeStruct(a.shape, a.d...  3.61 us

profile of v3, /device:TPU:1, one launch (start us, length us, event | category | flops | bytes accessed | tf_op | source)
XLA Modules:
  0.0 149.8 jit_solution(18375849210316343608)
XLA Ops:
  0.6 145.4 %shard_map.93 = (bf16[16,7168]{1,0:T(8,128)(2,1)}, f32[8,16]{1,0:T(8,128)}, bf16[896,1024]{1,0:T(8,128)(2,1)}, bf16[1024,896]{1,0:T(8,128)(2,1)}) custom-call(bf16[16,7168]{1,0:T(8,128)(2,1)} %tok_h.1, bf16[16,7168]{1,0:T(8,128)(2,1)} %go_h.1, s32[8,16]{1,0:T(8,128)} %bitcast.9, bf16[8,16]{1,0:T(8,128)(2,1)} %bitcast.10, bf16[896,1024]{1,0:T(8,128)(2,1)} %bitcast.7, ...), custom_call_target="tpu_custom_call" | custom-call | tf_op jit(solution)/shard_map/pallas_call | solution.py:512
  146.1 3.6 %shard_map.94 = (bf16[16,7168]{1,0:T(8,128)(2,1)}, f32[8,16]{1,0:T(8,128)}, bf16[896,1024]{1,0:T(8,128)(2,1)}, bf16[1024,896]{1,0:T(8,128)(2,1)}) custom-call(bf16[16,7168]{1,0:T(8,128)(2,1)} %get-tuple-element.12.refs_0_, f32[8,16]{1,0:T(8,128)} %get-tuple-element.13.refs_1_, bf16[896,1024]{1,0:T(8,128)(2,1)} %get-tuple-element.14.refs_2_, ...), custom_call_target="tpu_custom_call" | custom-call | tf_op jit(solution)/shard_map/pallas_call | solution.py:563
